TPU v7x, 256 devices: a whole 4x4x8 slice. The times are simulated.
256 devices in a mesh: tm: 32 (over x, z_lo, core), height: 8 (over y, z_hi).
Axes of the slice: x: 4, y: 4, z: 8 (z_hi: 2, z_lo: 4; z = z_hi * 4 + z_lo), core: 2. Of those that a mesh axis runs over, the one named last changes fastest.
Arguments:
- feats: bfloat16 [96, 16, 96, 192], P('tm', 'height'), may hold values from -6 to 6
- conv_weight: bfloat16 [3, 3, 3, 192, 192], replicated, may hold values from -0.078125 to 0.078125
- conv_bias: float32 [192], replicated, may hold values from -3 to 3
- patch_weight: bfloat16 [768, 1536], replicated, may hold values from -0.21875 to 0.21875
- patch_bias: float32 [1536], replicated, may hold values from -3 to 3
- time_weight: float32 [256, 4608], replicated, may hold values from -0.375 to 0.375
- qkv_weight: bfloat16 [3, 1536, 1024], P(None, None, 'height')
- out_weight: bfloat16 [1024, 1536], P('height'), may hold values from -0.1875 to 0.1875
- steps_index: int32 [32], P('tm'), may hold values from 0 to 999
- lookback: int32 [32], P('tm'), may hold values from 0 to 8, as said below
Outputs:
- refined: bfloat16 [96, 8, 48, 1536], P('tm', 'height')
Inputs may be any that keep to these rules, and one draw needn't show every extreme that they name: lookback of group k is at most k; the last group looks back 8 groups.
All inputs are finite; a program needn't handle non-finite values.
Results may differ from a plain program's by a relative error of at most 0.018.
Values may be sent and summed in bfloat16 or wider, within the bound.
A program may use at most 128 MiB of HBM per device.

v0:
```python
import math

import jax
import jax.numpy as jnp
from jax import lax
from jax.experimental import pallas as pl
from jax.experimental.pallas import tpu as pltpu
from jax.sharding import PartitionSpec as P

HD = 128
WIN = 8
D = 1536
CC = 192
FREQ = 256
ROW = 144
PIECE = 2 * ROW
HALF = 4 * ROW
NTOK = 8 * ROW
NEG = -1e30
MESH = pl.DeviceIdType.MESH
F32 = jnp.float32
BF16 = jnp.bfloat16


def kernel(
    feats, conv_w, conv_b, patch_w, patch_b, time_w, qkv_w, out_w, steps, lookback,
    out,
    own_rows, got_rows, fp, cw, pw, tw, wq, wo, ow, conv_acc, act, pat, tok, mod, q_ref, q_cols, kv, kv_far, acc, col_max, col_sum, obuf, mix,
    load_sem, z_send, z_recv, halo_send, halo_recv, pat_send, pat_recv, win_send, win_recv, fwd_send, mate_send,
    wo_sem, far_send, ow_send, ow_recv, share_send, share_recv, mix_send, mix_recv,
):
    tm = lax.axis_index("tm")
    h = lax.axis_index("height")
    x = tm // 8
    zl = (tm // 2) % 4
    c = tm % 2
    y = h // 2
    zh = h % 2

    def dev(x_, zl_, c_, y_, zh_):
        return (x_ * 8 + zl_ * 2 + c_, y_ * 2 + zh_)

    def remote(src, dst, send, recv, to):
        return pltpu.make_async_remote_copy(
            src_ref=src, dst_ref=dst, send_sem=send, recv_sem=recv, device_id=to, device_id_type=MESH
        )

    mine, theirs = 1 + 2 * zh, 3 - 2 * zh
    loads = [
        pltpu.make_async_copy(feats, fp.at[pl.ds(2, 3), pl.ds(mine, 2)], load_sem.at[0]),
        pltpu.make_async_copy(conv_w, cw, load_sem.at[1]),
        pltpu.make_async_copy(patch_w, pw, load_sem.at[2]),
        pltpu.make_async_copy(time_w, tw, load_sem.at[3]),
    ]
    for part in range(3):
        loads.append(
            pltpu.make_async_copy(qkv_w.at[part], wq.at[:, pl.ds(part * HD, HD)], load_sem.at[4 + part])
        )
    loads.append(pltpu.make_async_copy(out_w, ow.at[h], load_sem.at[7]))
    for cp in loads:
        cp.start()

    tm_next, tm_prev = (tm + 1) % 32, (tm + 31) % 32
    h_up, h_down = ((y + 1) % 4) * 2 + zh, ((y + 3) % 4) * 2 + zh
    partners = [(tm, (h + k) % 8) for k in range(1, 8)]
    partners += [(t, r) for t in (tm_next, tm_prev) for r in (h_down, h, h_up)]
    partners += [dev(x, (zl + k) % 4, c, y, zh) for k in (1, 3)]
    partners += [dev((x + k) % 4, zl, c, y, zh) for k in (1, 3)]
    partners += [dev(x, zl, 1 - c, y, zh)]
    partners += [dev(x, (zl + k) % 4, c, y, 1 - zh) for k in (1, 2, 3)]
    partners += [dev((x + k) % 4, 3 - zl, c, y, 1 - zh) for k in (1, 3)]
    barrier = pltpu.get_barrier_semaphore()
    for to in partners:
        pl.semaphore_signal(barrier, inc=1, device_id=to, device_id_type=MESH)

    loads[0].wait()
    for f in range(3):
        own_rows[f] = jnp.concatenate([fp[2 + f, mine], fp[2 + f, mine + 1]], axis=1)
    pl.semaphore_wait(barrier, len(partners))

    z_copies = {
        f: remote(own_rows.at[f], got_rows.at[f], z_send.at[f], z_recv.at[f], (tm, y * 2 + 1 - zh)) for f in (1, 2, 0)
    }
    for cp in z_copies.values():
        cp.start()

    def passing(rows, edge, to_up, first):
        to_h = to_up * h_up + (1 - to_up) * h_down
        at = 5 * (1 - to_up)
        late = fp.at[pl.ds(3, 2), pl.ds(edge, 1)]
        return [
            remote(
                fp.at[pl.ds(3, 2), pl.ds(rows, 2)], fp.at[pl.ds(0, 2), pl.ds(rows, 2)],
                halo_send.at[first], halo_recv.at[rows // 2], (tm_next, h),
            ),
            remote(late, fp.at[pl.ds(0, 2), pl.ds(at, 1)], halo_send.at[first + 1], halo_recv.at[2 + to_up], (tm_next, to_h)),
            remote(
                fp.at[pl.ds(2, 3), pl.ds(edge, 1)], fp.at[pl.ds(2, 3), pl.ds(at, 1)],
                halo_send.at[first + 2], halo_recv.at[4 + to_up], (tm, to_h),
            ),
        ]

    halo = passing(mine, 1 + 3 * zh, zh, 0)
    for cp in halo:
        cp.start()

    index = lax.broadcasted_iota(jnp.int32, (FREQ // 2, 128), 0)
    coarse = jnp.zeros((FREQ // 2, 128), F32)
    fine = jnp.zeros((FREQ // 2, 128), F32)
    for i in range(16):
        coarse = jnp.where(index // 8 == i, math.exp(-math.log(10000.0) * i / 16), coarse)
    for i in range(8):
        fine = jnp.where(index % 8 == i, math.exp(-math.log(10000.0) * i / 128), fine)
    angle = steps[0].astype(F32) * (coarse * fine)
    embedding = jnp.concatenate([jnp.cos(angle), jnp.sin(angle)], axis=0)
    loads[3].wait()
    for part in range(3):
        for tile in range(D // 128):
            lane = part * D + tile * 128
            mod[part : part + 1, tile * 128 : (tile + 1) * 128] = jnp.sum(
                tw[:, lane : lane + 128] * embedding, axis=0, keepdims=True
            )

    conv_acc[...] = jnp.zeros_like(conv_acc)
    loads[1].wait()
    halo_more = passing(theirs, 1 + 3 * (1 - zh), 1 - zh, 3)
    for f, cp in z_copies.items():
        cp.wait_recv()
        both = got_rows[f]
        fp[2 + f, theirs] = both[:, :CC]
        fp[2 + f, theirs + 1] = both[:, CC:]
        if f == 2:
            halo_more[0].start()
            halo_more[1].start()
    halo_more[2].start()

    at_end = (zl % 3) == 0
    ow_near = dev(x, 3 * (1 - zl // 3), c, y, 1 - zh)
    ow_far = dev(x, 1 + (1 - zl // 3), c, y, 1 - zh)
    for cp in loads[4:7]:
        cp.wait()
    wo_rows = pl.ds(pl.multiple_of(c * (D // 2), D // 2), D // 2)
    wo_rest = pl.ds(pl.multiple_of((1 - c) * (D // 2), D // 2), D // 2)
    wo_copy = remote(wq.at[wo_rows, pl.ds(HD, 2 * HD)], wo.at[wo_rows], wo_sem.at[0], wo_sem.at[1], ow_near)
    wo_share = remote(wo.at[wo_rows], wo.at[wo_rows], wo_sem.at[2], wo_sem.at[3], dev(x, zl, 1 - c, y, zh))

    @pl.when(at_end)
    def _():
        wo_copy.start()

    def tap(a, b, f, nf, r, nr):
        rows = fp[f + a : f + a + nf, r + b : r + b + nr].reshape(nf * nr * 96, CC)
        for e in range(3):
            term = jnp.dot(rows, cw[a, b, e], preferred_element_type=F32)
            conv_acc[e, f : f + nf, r : r + nr, 8:104] += term.reshape(nf, nr, 96, CC)

    for a in range(3):
        for b in range(3):
            tap(a, b, 2 - a, 1 + a, 1 if b == 0 else 0, 4 if b == 1 else 3)

    def halo_wait(f, nf, r, nr, sem):
        spot = fp.at[pl.ds(f, nf), pl.ds(r, nr)]
        remote(spot, spot, halo_send.at[0], halo_recv.at[sem], (tm_next, h)).wait_recv()

    halo_wait(0, 2, 1, 2, 0)
    halo_wait(0, 2, 3, 2, 1)
    halo_wait(0, 2, 5, 1, 2)
    halo_wait(0, 2, 0, 1, 3)
    halo_wait(2, 3, 5, 1, 4)
    halo_wait(2, 3, 0, 1, 5)

    @pl.when(y == 0)
    def _():
        fp[:, 0:1] = jnp.zeros((5, 1, 96, CC), BF16)

    @pl.when(y == 3)
    def _():
        fp[:, 5:6] = jnp.zeros((5, 1, 96, CC), BF16)

    @pl.when(tm == 0)
    def _():
        fp[0:2] = jnp.zeros((2, 6, 96, CC), BF16)

    for a in range(3):
        for b in range(3):
            if a < 2:
                tap(a, b, 0, 2 - a, 0, 4)
            if b != 1:
                tap(a, b, 2 - a, 1 + a, 0 if b == 0 else 3, 1)
    for f in range(3):
        for r in range(4):
            v = conv_acc[0, f, r, 7:103] + conv_acc[1, f, r, 8:104] + conv_acc[2, f, r, 9:105] + conv_b[...]
            v = v / (1.0 + jnp.exp(-v))
            act[0, f, r] = v[:, 0:128]
            act[1, f, r, :, 0:64] = v[:, 128:192]
    for f in range(3):
        for row in range(2):
            pieces = []
            for u in range(2):
                for w in range(2):
                    columns = pl.ds(w, 48, stride=2)
                    r = 2 * row + u
                    pieces += [act[0, f, r, columns, :], act[1, f, r, columns, :][:, :64]]
            pat[row, pl.ds(48 * f, 48)] = jnp.concatenate(pieces, axis=1).astype(BF16)

    def pat_copy(src, dst, sem, to):
        return remote(pat.at[src], pat.at[dst], pat_send.at[sem], pat_recv.at[dst], (tm, to))

    pat_copies = [
        pat_copy(0, 2, 0, h_up),
        pat_copy(1, 3, 1, h_down),
        pat_copy(1, 4, 2, h_up),
        pat_copy(0, 5, 3, h_down),
    ]
    pat_onward = [pat_copy(2, 6, 4, h_up), pat_copy(3, 7, 5, h_down)]
    order = [(0, 0), (0, 1), (3, 0), (1, 1), (3, 1), (1, 0), (2, 0), (2, 1)]
    for cp in pat_copies:
        cp.start()
    loads[2].wait()

    @pl.when(at_end)
    def _():
        wo_copy.wait_recv()
        wo_share.start()
        remote(wo.at[wo_rest], wo.at[wo_rest], wo_sem.at[2], wo_sem.at[3], dev(x, zl, 1 - c, y, zh)).wait_recv()

    def pat_wait(slot):
        remote(pat.at[slot], pat.at[slot], pat_send.at[0], pat_recv.at[slot], (tm, h_up)).wait_recv()

    own_part = pl.ds(pl.multiple_of(c * (HD // 2), HD // 2), HD // 2)
    ow_z = [
        remote(ow.at[h, own_part], ow.at[h, own_part], ow_send.at[6 + i], ow_recv.at[h], to)
        for i, to in enumerate((ow_near, ow_far))
    ]
    loads[7].wait()

    shift_row = mod[0:1, :]
    scale_row = 1.0 + mod[1:2, :]
    q_scale = HD ** (-0.5) * math.log2(math.e)

    def project(group):
        patches = pat[2 * group : 2 * group + 2].reshape(PIECE, 4 * CC)
        tokens = (jnp.dot(patches, pw[...], preferred_element_type=F32) + patch_b[...]).astype(BF16)
        if group == 0:

            @pl.when(zh == 0)
            def _():
                tok[...] = tokens[:ROW]

            @pl.when(zh == 1)
            def _():
                tok[...] = tokens[ROW:]

        wide = tokens.astype(F32)
        centered = wide - jnp.mean(wide, axis=-1, keepdims=True)
        variance = jnp.mean(centered * centered, axis=-1, keepdims=True)
        normed = (centered * lax.rsqrt(variance + 1e-06) * scale_row + shift_row).astype(BF16)
        qkv = jnp.dot(normed, wq[...], preferred_element_type=F32)
        rows = pl.ds(group * PIECE, PIECE)
        q_ref[rows, :] = (qkv[:, 0:HD] * q_scale).astype(BF16)
        kv[0, 0, rows, :] = qkv[:, HD : 2 * HD].astype(BF16)
        kv[0, 1, rows, :] = qkv[:, 2 * HD :].astype(BF16)

        @pl.when(at_end)
        def _():
            other = jnp.dot(normed, wo[...], preferred_element_type=F32).astype(BF16)
            kv_far[0, rows, :] = other[:, :HD]
            kv_far[1, rows, :] = other[:, HD:]

    def half_rows(g):
        return pl.ds(pl.multiple_of(g * HALF, HALF), HALF)

    def half_of(slot, g):
        return kv.at[slot, :, half_rows(g), :]

    def piece_of(slot, p):
        return kv.at[slot, :, pl.ds(pl.multiple_of(p * PIECE, PIECE), PIECE), :]

    z_next = dev(x, (zl + 1) % 4, c, y, zh)
    z_prev = dev(x, (zl + 3) % 4, c, y, zh)
    x_next = dev((x + 1) % 4, zl, c, y, zh)
    mate = dev(x, zl, 1 - c, y, zh)

    win_copies = []
    end_to = dev((x + zl // 3) % 4, 3 * (1 - zl // 3), c, y, 1 - zh)
    end_slot = 3 - 2 * (zl // 3)

    def send_own(p):
        up = remote(piece_of(0, p), piece_of(1, p), win_send.at[p], win_recv.at[1, p], z_next)
        across = remote(piece_of(0, p), piece_of(4, p), win_send.at[4 + p], win_recv.at[4, p], x_next)
        far = remote(
            kv_far.at[:, pl.ds(p * PIECE, PIECE)], piece_of(end_slot, p), far_send.at[p], win_recv.at[end_slot, p], end_to
        )
        across.start()

        @pl.when(zl < 3)
        def _():
            up.start()

        @pl.when(at_end)
        def _():
            far.start()

        win_copies.append((up, across, far))

    def passing_on(d, p):
        up = remote(piece_of(d, p), piece_of((d + 1) % 5, p), fwd_send.at[d - 1, p], win_recv.at[(d + 1) % 5, p], z_next)
        down = remote(piece_of(d, p), piece_of(d - 1, p), fwd_send.at[d - 1, p], win_recv.at[d - 1, p], z_prev)
        middle = jnp.logical_and(zl > 0, zl < 3)
        goes_up = jnp.logical_and(d == 1, middle)
        goes_down = jnp.logical_or(jnp.logical_and(d == 4, zl > 0), jnp.logical_and(d == 3, middle))
        return up, down, goes_up, goes_down

    def pass_on(d, p):
        remote(piece_of(0, p), piece_of(d, p), fwd_send.at[0, 0], win_recv.at[d, p], mate).wait_recv()
        up, down, goes_up, goes_down = passing_on(d, p)

        @pl.when(goes_up)
        def _():
            up.start()

        @pl.when(goes_down)
        def _():
            down.start()

    def share_copy(d, g):
        src = c * d + (1 - c) * (d % 4)
        dst = 4 + c * d + (1 - c) * (d % 4 + 1)
        return remote(half_of(src, g), half_of(dst, g), mate_send.at[d - 1, g], win_recv.at[dst, g], mate)

    project(0)
    send_own(0)

    @pl.when(at_end)
    def _():
        for cp in ow_z:
            cp.start()

    pat_wait(2)
    pat_onward[0].start()
    pat_wait(3)
    pat_onward[1].start()
    project(1)
    send_own(1)
    pat_wait(4)
    pat_wait(5)
    project(2)
    send_own(2)
    for d in (1, 4):
        pass_on(d, 0)
    pat_wait(6)
    pat_wait(7)
    project(3)
    send_own(3)
    for d in (1, 4):
        pass_on(d, 1)
        share_copy(d, 0).start()
    pass_on(3, 0)

    def ow_sends(row, first):
        part = ow.at[row, own_part]
        return [
            remote(part, part, ow_send.at[first + k], ow_recv.at[row], (tm, ((y + k + 1) % 4) * 2 + zh)) for k in (0, 2, 1)
        ]

    def ow_wait(row):
        part = ow.at[row, own_part]
        remote(part, part, ow_send.at[0], ow_recv.at[row], (tm, h_up)).wait_recv()

    def ow_share(row):
        part = ow.at[row, own_part]
        return remote(part, part, share_send.at[row], share_recv.at[row], mate)

    h_other = y * 2 + 1 - zh
    ow_copies = ow_sends(h, 0) + ow_sends(h_other, 3)
    for cp in ow_copies[:3]:
        cp.start()
    others = [h_other] + [((y + k) % 4) * 2 + half for k in range(1, 4) for half in range(2)]

    q_cols[...] = q_ref[...].astype(F32).T.astype(BF16)
    acc[...] = jnp.zeros_like(acc)
    col_sum[...] = jnp.zeros_like(col_sum)
    col_max[...] = jnp.full_like(col_max, NEG)

    def attend(slot, g, back):
        penalty = jnp.where(back <= lookback[0], 0.0, 1e30)
        values = kv[slot, 1, half_rows(g), :].T
        scores = jnp.dot(kv[slot, 0, half_rows(g), :], q_cols[...], preferred_element_type=F32)
        old = col_max[...]
        new = jnp.maximum(old, jnp.max(scores, axis=0, keepdims=True) - penalty)
        probs = jnp.exp2(scores - (new + penalty))
        shrink = jnp.exp2(old - new)
        col_max[...] = new
        col_sum[...] = col_sum[...] * shrink + jnp.sum(probs, axis=0, keepdims=True)
        acc[...] = acc[...] * shrink + jnp.dot(values, probs.astype(BF16), preferred_element_type=F32)

    arrivals = [(1, 0), (4, 0), (3, 0), (1, 1), (4, 1), (3, 1), (2, 0), (2, 1)]
    code = sum(((d - 1) * 2 + g) * 8**i for i, (d, g) in enumerate(arrivals))
    steps_of = {
        0: ([(1, 2), (4, 2)], []),
        1: ([(3, 1), (1, 3), (4, 3)], [(3, 0), (1, 1), (4, 1)]),
        2: ([(3, 2)], []),
        3: ([(3, 3)], [(3, 1)]),
        4: ([(2, 0), (2, 1)], [(2, 0)]),
        6: ([(2, 2), (2, 3)], [(2, 1)]),
    }

    def event(n, code):
        for at, (passed, shared) in steps_of.items():

            @pl.when(n == at)
            def _(passed=passed, shared=shared):
                for d, p in passed:
                    pass_on(d, p)
                for d, g in shared:
                    share_copy(d, g).start()

        @pl.when(n == 3)
        def _():
            ow_wait(h_other)
            for cp in ow_copies[3:]:
                cp.start()

        @pl.when(n == 7)
        def _():
            for row in others[1:]:
                ow_wait(row)
            for row in others:
                ow_share(row).start()

        first = (8 - n) // 8
        digit = code % 8
        d = (1 - first) * (digit // 2 + 1)
        g = (1 - first) * (digit % 2)
        got = 4 + (1 - c) * d + c * (d % 4 + 1)

        def one(k, _):
            @pl.when(jnp.logical_and(n > 0, k == 1))
            def _():
                remote(half_of(0, g), half_of(got, g), mate_send.at[0, 0], win_recv.at[got, g], mate).wait_recv()

            slot = (1 - k) * d + k * (1 - first) * got
            back = jnp.where(slot <= 4, 2 * slot, 2 * slot - 9)
            attend(slot, g + k * first, back)
            return 0

        lax.fori_loop(0, 2, one, 0)
        return first * code + (1 - first) * (code // 8)

    lax.fori_loop(0, 9, event, code)

    def mix_copy(s):
        to = ((y + order[s][0]) % 4) * 2 + order[s][1]
        return to, remote(obuf.at[s], mix.at[h], mix_send.at[s], mix_recv.at[h], (tm, to))

    all_out = (acc[...] / col_sum[...]).T.astype(BF16)
    for s in range(8):
        heads_out = all_out[s * ROW : (s + 1) * ROW]
        obuf[s] = heads_out
        to, cp = mix_copy(s)

        @pl.when(to == h)
        def _(heads_out=heads_out):
            mix[h] = heads_out

        @pl.when(to != h)
        def _(cp=cp):
            cp.start()

    for row in others:
        part = ow.at[row, pl.ds(pl.multiple_of((1 - c) * (HD // 2), HD // 2), HD // 2)]
        remote(part, part, share_send.at[row], share_recv.at[row], mate).wait_recv()
    for k in range(1, 8):
        r = (h + k) % 8
        remote(obuf.at[0], mix.at[r], mix_send.at[0], mix_recv.at[r], (tm, h_up)).wait_recv()
    heads = jnp.concatenate([mix[i] for i in range(8)], axis=1)
    attended = jnp.dot(heads, ow[...].reshape(8 * HD, D), preferred_element_type=F32)
    refined = (tok[...].astype(F32) + mod[2:3, :] * attended).astype(BF16)
    out[...] = refined.reshape(3, 1, 48, D)

    for cp in halo + halo_more + list(z_copies.values()) + pat_copies + pat_onward + ow_copies:
        cp.wait_send()
    for row in others:
        ow_share(row).wait_send()

    @pl.when(at_end)
    def _():
        for cp in ow_z + [wo_copy, wo_share] + [far for _, _, far in win_copies]:
            cp.wait_send()

    for up, across, _ in win_copies:
        across.wait_send()

        @pl.when(zl < 3)
        def _(up=up):
            up.wait_send()

    def drain(i, _):
        d = i // 4 + 1
        up, down, goes_up, goes_down = passing_on(d, i % 4)

        @pl.when(goes_up)
        def _():
            up.wait_send()

        @pl.when(goes_down)
        def _():
            down.wait_send()

        return 0

    lax.fori_loop(0, 16, drain, 0)
    for d in range(1, 5):
        for g in range(2):
            share_copy(d, g).wait_send()

    for s in range(8):
        to, cp = mix_copy(s)

        @pl.when(to != h)
        def _(cp=cp):
            cp.wait_send()


def on_device(
    feats, conv_weight, conv_bias, patch_weight, patch_bias, time_weight, qkv_weight, out_weight, steps_index, lookback
):
    vmem = pl.BlockSpec(memory_space=pltpu.VMEM)
    smem = pl.BlockSpec(memory_space=pltpu.SMEM)
    hbm = pl.BlockSpec(memory_space=pl.ANY)
    dma = pltpu.SemaphoreType.DMA
    return pl.pallas_call(
        kernel,
        out_shape=jax.ShapeDtypeStruct((3, 1, 48, D), BF16),
        in_specs=[hbm, hbm, vmem, hbm, vmem, hbm, hbm, hbm, smem, smem],
        out_specs=vmem,
        scratch_shapes=[
            pltpu.VMEM((3, 96, 2 * CC), BF16),
            pltpu.VMEM((3, 96, 2 * CC), BF16),
            pltpu.VMEM((5, 6, 96, CC), BF16),
            pltpu.VMEM((3, 3, 3, CC, CC), BF16),
            pltpu.VMEM((4 * CC, D), BF16),
            pltpu.VMEM((FREQ, 3 * D), F32),
            pltpu.VMEM((D, 3 * HD), BF16),
            pltpu.VMEM((D, 2 * HD), BF16),
            pltpu.VMEM((8, HD, D), BF16),
            pltpu.VMEM((3, 3, 4, 112, CC), F32),
            pltpu.VMEM((2, 3, 4, 96, 128), F32),
            pltpu.VMEM((8, ROW, 4 * CC), BF16),
            pltpu.VMEM((ROW, D), BF16),
            pltpu.VMEM((3, D), F32),
            pltpu.VMEM((NTOK, HD), BF16),
            pltpu.VMEM((HD, NTOK), BF16),
            pltpu.VMEM((9, 2, NTOK, HD), BF16),
            pltpu.VMEM((2, NTOK, HD), BF16),
            pltpu.VMEM((HD, NTOK), F32),
            pltpu.VMEM((1, NTOK), F32),
            pltpu.VMEM((1, NTOK), F32),
            pltpu.VMEM((8, ROW, HD), BF16),
            pltpu.VMEM((8, ROW, HD), BF16),
            dma((8,)),
            dma((3,)),
            dma((3,)),
            dma((6,)),
            dma((6,)),
            dma((6,)),
            dma((8,)),
            dma((8,)),
            dma((9, 4)),
            dma((4, 4)),
            dma((4, 2)),
            dma((4,)),
            dma((4,)),
            dma((8,)),
            dma((8,)),
            dma((8,)),
            dma((8,)),
            dma((8,)),
            dma((8,)),
        ],
        compiler_params=pltpu.CompilerParams(
            collective_id=0, has_side_effects=True, vmem_limit_bytes=56 * 1024 * 1024
        ),
        name="block",
    )(
        feats, conv_weight, conv_bias, patch_weight, patch_bias, time_weight,
        qkv_weight, out_weight, steps_index, lookback,
    )


def solution(mesh):
    in_specs = (
        P("tm", "height", None, None),
        P(),
        P(),
        P(),
        P(),
        P(),
        P(None, None, "height"),
        P("height", None),
        P("tm"),
        P("tm"),
    )
    out_specs = P("tm", "height", None, None)
    return jax.shard_map(
        on_device, mesh=mesh, in_specs=in_specs, out_specs=out_specs, check_vma=False
    )
```

profile of v0, /device:TPU:8, one launch (start us, length us, event | category | flops | bytes accessed | tf_op | source)
XLA Modules:
  0.0 99.9 jit_solution(8813955870101131062)
XLA Ops:
  1.3 96.7 %block.1 = bf16[3,1,48,1536]{3,2,1,0:T(8,128)(2,1)} custom-call(bf16[3,2,96,192]{3,2,1,0:T(8,128)(2,1)} %feats.1, bf16[3,3,3,192,192]{4,3,2,1,0:T(8,128)(2,1)} %conv_w.1, f32[192]{0:T(256)} %conv_b.1, bf16[768,1536]{1,0:T(8,128)(2,1)} %patch_w.1, f32[1536]{0:T(1024)} %patch_b.1, f32[256,4608]{1,0:T(8,128)} %time_w.1, bf16[3,1536,128]{2,1,0:T(8,128)(2,1)} %qkv_w.1, ...), custom_call_target="tpu_custom_call" | custom-call | tf_op jit(solution)/shard_map/block/pallas_call | solution.py:532
  98.0 1.8 %copy.14 = bf16[3,1,48,1536]{3,2,1,0:T(8,128)(2,1)} copy(bf16[3,1,48,1536]{3,2,1,0:T(8,128)(2,1)} %block.1) | data formatting | bytes 884736
where the time goes:
time: 101 us; the launch traced here: 99.9 us
  Pallas kernels  96.7 us (96%)
  local copies, waits for them, and re-layouts  1.8 us (2%)
  between operations  1.31 us (1%)
    pallas_call x1, Pallas kernels, on_device(): pl.pallas_call(kernel, out_shape=jax.ShapeDtypeStruct((3, 1, 48, D), BF16...  96.7 us

commit v1 on v0

--- a/solution.py
+++ b/solution.py
@@ -398,23 +398,15 @@
     code = sum(((d - 1) * 2 + g) * 8**i for i, (d, g) in enumerate(arrivals))
     steps_of = {
         0: ([(1, 2), (4, 2)], []),
-        1: ([(3, 1), (1, 3), (4, 3)], [(3, 0), (1, 1), (4, 1)]),
-        2: ([(3, 2)], []),
-        3: ([(3, 3)], [(3, 1)]),
-        4: ([(2, 0), (2, 1)], [(2, 0)]),
-        6: ([(2, 2), (2, 3)], [(2, 1)]),
+        1: ([(3, 1)], [(3, 0)]),
+        2: ([(1, 3), (4, 3)], [(1, 1), (4, 1)]),
+        3: ([(3, 2)], []),
+        5: ([(3, 3)], [(3, 1)]),
+        8: ([(2, 0), (2, 1)], [(2, 0)]),
+        12: ([(2, 2), (2, 3)], [(2, 1)]),
     }
 
     def event(n, code):
-        for at, (passed, shared) in steps_of.items():
-
-            @pl.when(n == at)
-            def _(passed=passed, shared=shared):
-                for d, p in passed:
-                    pass_on(d, p)
-                for d, g in shared:
-                    share_copy(d, g).start()
-
         @pl.when(n == 3)
         def _():
             ow_wait(h_other)
@@ -435,6 +427,15 @@
         got = 4 + (1 - c) * d + c * (d % 4 + 1)
 
         def one(k, _):
+            for at, (passed, shared) in steps_of.items():
+
+                @pl.when(2 * n + k == at)
+                def _(passed=passed, shared=shared):
+                    for d, p in passed:
+                        pass_on(d, p)
+                    for d, g in shared:
+                        share_copy(d, g).start()
+
             @pl.when(jnp.logical_and(n > 0, k == 1))
             def _():
                 remote(half_of(0, g), half_of(got, g), mate_send.at[0, 0], win_recv.at[got, g], mate).wait_recv()

time: 101 us -> 101 us (level); the launches traced: 99.9 us -> 101 us
  Pallas kernels: 96.7 us -> 98.2 us
    pallas_call x1, Pallas kernels: 96.7 us -> 98.2 us  [on_device(): pl.pallas_call(kernel, out_shape=jax.ShapeDtypeStruct((3, 1, 48, D), BF16...]
where the time goes in v1:
time: 101 us
  Pallas kernels  98.2 us (97%)
  local copies, waits for them, and re-layouts  1.8 us (2%)
  between operations  1.31 us (1%)
    pallas_call x1, Pallas kernels, on_device(): pl.pallas_call(kernel, out_shape=jax.ShapeDtypeStruct((3, 1, 48, D), BF16...  98.2 us

profile of v1, /device:TPU:8, one launch (start us, length us, event | category | flops | bytes accessed | tf_op | source)
XLA Modules:
  0.0 101.3 jit_solution(6622432674813094563)
XLA Ops:
  1.3 98.2 %block.1 = bf16[3,1,48,1536]{3,2,1,0:T(8,128)(2,1)} custom-call(bf16[3,2,96,192]{3,2,1,0:T(8,128)(2,1)} %feats.1, bf16[3,3,3,192,192]{4,3,2,1,0:T(8,128)(2,1)} %conv_w.1, f32[192]{0:T(256)} %conv_b.1, bf16[768,1536]{1,0:T(8,128)(2,1)} %patch_w.1, f32[1536]{0:T(1024)} %patch_b.1, f32[256,4608]{1,0:T(8,128)} %time_w.1, bf16[3,1536,128]{2,1,0:T(8,128)(2,1)} %qkv_w.1, ...), custom_call_target="tpu_custom_call" | custom-call | tf_op jit(solution)/shard_map/block/pallas_call | solution.py:533
  99.5 1.8 %copy.14 = bf16[3,1,48,1536]{3,2,1,0:T(8,128)(2,1)} copy(bf16[3,1,48,1536]{3,2,1,0:T(8,128)(2,1)} %block.1) | data formatting | bytes 884736
